TPU v7x, 32 devices: a whole 2x2x4 slice. The times are simulated.
32 devices in a mesh: scen: 8 (over z, x), fac: 4 (over y, core).
Axes of the slice: x: 2, y: 2, z: 4, core: 2. Of those that a mesh axis runs over, the one named last changes fastest.
Arguments:
- scenario_draws: bfloat16 [8192, 4096], P('scen'), may hold values from -6 to 6
- cholesky: bfloat16 [4096, 4096], P('scen', 'fac'), may hold values from -1.5 to 1.5, as said below
- exposures: bfloat16 [4096, 4096], P('fac'), may hold values from -0.09375 to 0.09375
- drift: float32 [4096], P('fac'), may hold values from -3 to 3
Outputs:
- covariance: float32 [4096, 4096], P('scen', 'fac')
- expected: float32 [4096], P('fac')
Inputs may be any that keep to these rules, and one draw needn't show every extreme that they name: cholesky is lower triangular (zero above the diagonal) with diagonal entries of 0.5 to 1.5.
All inputs are finite; a program needn't handle non-finite values.
Results may differ from a plain program's by a relative error of at most 0.0013.
Values may be sent and summed in bfloat16 or wider, within the bound.
A program may use at most 128 MiB of HBM per device.

v0:
```python
import jax
import jax.numpy as jnp
from jax import lax
from jax.sharding import PartitionSpec as P

BF16, F16, F32 = jnp.bfloat16, jnp.float16, jnp.float32
CHUNKS = 2


def flip(size, bit):
    return [(i, i ^ bit) for i in range(size)]


def swap(value, axis, bit):
    return lax.ppermute(value, axis, flip(lax.axis_size(axis), bit))


def rows_dot(a, b):
    return lax.dot_general(a, b, (((0,), (0,)), ((), ())), preferred_element_type=F32)


def cols_dot(a, b):
    return lax.dot_general(a, b, (((1,), (1,)), ((), ())), preferred_element_type=F32)


def on_device(scenario_draws, cholesky, exposures, drift):
    n_scen, n_fac = lax.axis_size("scen"), lax.axis_size("fac")
    si, fi = lax.axis_index("scen"), lax.axis_index("fac")
    nz = n_scen // 2
    zi, xi = si // 2, si % 2
    count = scenario_draws.shape[0]
    own = exposures.shape[0]
    desks = own * n_fac
    block = desks // n_scen
    per_fac = own // block // 2
    factors = cholesky.shape[1]
    total = count * n_scen
    plane = 2 * count

    depth = cholesky.shape[0]

    def along_z(value, pairs):
        return lax.ppermute(
            value, "scen", [(2 * a + x, 2 * b + x) for a, b in pairs for x in range(2)]
        )

    def across_x(value, zs):
        return lax.ppermute(value, "scen", [(2 * z + x, 2 * z + 1 - x) for z in zs for x in range(2)])

    above, below = [cholesky], [cholesky]
    for t in range(1, nz):
        above.append(along_z(above[-1], [(z - 1, z) for z in range(t, nz)]))
        below.append(along_z(below[-1], [(z + 1, z) for z in range(nz - t)]))
    chol = [(si, cholesky), (si ^ 1, swap(cholesky, "scen", 1))]
    far_above = [across_x(above[t], range(t, nz)) for t in range(1, nz)]
    far_below = [across_x(below[t], range(nz - t)) for t in range(1, nz)]
    for t in range(1, nz):
        home = 2 * ((zi - t + nz) % nz) + xi
        chol.append((home, jnp.where(zi >= t, above[t], below[nz - t])))
        chol.append((home ^ 1, jnp.where(zi >= t, far_above[t - 1], far_below[nz - t - 1])))
    lower = jnp.concatenate([piece for _, piece in chol], axis=0)
    turned = jnp.concatenate(
        [lax.dynamic_slice_in_dim(scenario_draws, home * depth, depth, 1) for home, _ in chol], axis=1
    )
    weights = [
        lax.dynamic_slice_in_dim(exposures, (fi ^ k) * factors, factors, 1) for k in range(n_fac)
    ]

    def own_parity(value):
        split = value.reshape(value.shape[0], per_fac, 2, block)
        return lax.dynamic_index_in_dim(split, xi, 2, keepdims=False).reshape(
            value.shape[0], per_fac * block
        )

    grams = [0.0] * n_fac
    sums, squares = [0.0, 0.0], [0.0, 0.0]
    step = count // CHUNKS
    for c in range(CHUNKS):
        draws = turned[c * step : (c + 1) * step]
        mixed = jnp.dot(draws, lower, preferred_element_type=F32)
        shocks = (mixed + drift[None, :]).astype(BF16)
        far = swap(shocks, "fac", 2)
        parts = [shocks, swap(shocks, "fac", 1), far, swap(far, "fac", 1)]
        acc = cols_dot(parts[0], weights[0])
        for k in range(1, n_fac):
            acc = acc + cols_dot(parts[k], weights[k])
        pnl = acc.astype(BF16)
        for side, piece in enumerate((pnl, swap(pnl, "scen", 1))):
            wide = piece.astype(F32)
            sums[side] = sums[side] + jnp.sum(wide, axis=0)
            squares[side] = squares[side] + jnp.sum(jnp.square(wide), axis=0)
            mine = own_parity(piece)
            across = swap(mine, "fac", 2)
            got = [mine, swap(mine, "fac", 1), across, swap(across, "fac", 1)]
            for k in range(n_fac):
                grams[k] = grams[k] + rows_dot(got[k], piece)

    largest = jnp.max(squares[0] + squares[1])
    stats = jnp.concatenate([sums[0] + sums[1], jnp.full((128,), largest)])
    around = [stats]
    for k in range(1, nz):
        pairs = [(2 * z + x, 2 * ((z + k) % nz) + x) for z in range(nz) for x in range(2)]
        around.append(lax.ppermute(stats, "scen", pairs))
    around = jnp.stack(around)
    by_z = jnp.stack(
        [
            lax.dynamic_index_in_dim(around, (zi - z + nz) % nz, 0, keepdims=False)
            for z in range(nz)
        ]
    )
    far = swap(by_z, "fac", 2)
    everyone = jnp.stack([by_z, swap(by_z, "fac", 1), far, swap(far, "fac", 1)])
    limit = jnp.max(everyone[:, :, own:]) * (1.01 * nz)
    power = jnp.floor(14.0 - jnp.log2(jnp.where(limit > 0, limit, 1.0)))
    scale = jnp.exp2(jnp.clip(power, -100.0, 100.0))

    col_sums = by_z[:, :own]
    row_sums = own_parity(everyone[:, :, :own].reshape(n_fac * nz, own)).reshape(
        n_fac, nz, per_fac, block
    )
    here = lax.dynamic_index_in_dim(row_sums, zi, 1, keepdims=False)
    col_mean = (sums[0] + sums[1]) / plane

    def block_of(array, z):
        z = jnp.clip(z, 0, nz - 1)
        return lax.dynamic_slice(
            array, (fi ^ (z // per_fac), z % per_fac) + (0,) * (array.ndim - 2), (1, 1) + array.shape[2:]
        ).reshape(array.shape[2:])

    parts = jnp.stack(
        [
            (grams[k] - here[k].reshape(-1)[:, None] * col_mean[None, :]) * scale
            for k in range(n_fac)
        ]
    ).reshape(n_fac, per_fac, block, own)

    mine = block_of(parts, zi)
    arrived = [None, None]
    for t in range(1, nz):
        for up in (0, 1):
            if up:
                pairs = [(z, z + 1) for z in range(t)]
                target = nz - t + zi
            else:
                pairs = [(nz - 1 - z, nz - 2 - z) for z in range(t)]
                target = zi + t - nz
            pairs = [(2 * a + x, 2 * b + x) for a, b in pairs for x in range(2)]
            value = block_of(parts, target)
            if arrived[up] is not None:
                value = value + arrived[up].astype(F32)
            arrived[up] = lax.ppermute(value.astype(F16), "scen", pairs)
    mine = (mine + arrived[0].astype(F32) + arrived[1].astype(F32)) / scale

    my_rows = jnp.stack([block_of(row_sums[:, z], zi) for z in range(nz)])
    col_total = jnp.sum(col_sums, axis=0)
    row_total = jnp.sum(my_rows, axis=0)
    fix = -row_total[:, None] * (col_total / total)[None, :]
    for z in range(nz):
        fix = fix + my_rows[z][:, None] * (col_sums[z] / plane)[None, :]
    return (mine + fix) / (total - 1), col_total / total


def solution(mesh):
    placed = (P("scen", None), P("scen", "fac"), P("fac", None), P("fac"))
    return jax.shard_map(
        on_device,
        mesh=mesh,
        in_specs=placed,
        out_specs=(P("scen", "fac"), P("fac")),
        check_vma=False,
    )
```

profile of v0, /device:TPU:0, one launch (start us, length us, event | category | flops | bytes accessed | tf_op | source)
XLA Modules:
  0.0 452.4 jit_solution(10659279356380722964)
XLA Ops:
  1.9 6.5 %collective-permute-start.1 = (bf16[512,1024]{1,0:T(8,128)(2,1)}, bf16[512,1024]{1,0:T(8,128)(2,1)}, u32[]{:S(2)}, u32[]{:S(2)}) collective-permute-start(bf16[512,1024]{1,0:T(8,128)(2,1)} %param.5), channel_id=1, source_target_pairs={{0,8},{4,12},{8,16},{12,20},{16,24},{20,28},{1,9},{5,13},{9,17},{1... | collective-permute-start | bytes 3145736 | tf_op jit(solution)/shard_map/ppermute | solution.py:43
  8.5 20.4 %collective-permute-done.2 = bf16[512,1024]{1,0:T(8,128)(2,1)S(1)} collective-permute-done((bf16[512,1024]{1,0:T(8,128)(2,1)}, bf16[512,1024]{1,0:T(8,128)(2,1)S(1)}, u32[]{:S(2)}, u32[]{:S(2)}) %collective-permute-start.2) | collective-permute-done | bytes 1048608 | tf_op jit(solution)/shard_map/ppermute | solution.py:43
  31.0 24.2 %collective-permute-done.3 = bf16[512,1024]{1,0:T(8,128)(2,1)S(1)} collective-permute-done((bf16[512,1024]{1,0:T(8,128)(2,1)S(1)}, bf16[512,1024]{1,0:T(8,128)(2,1)S(1)}, u32[]{:S(2)}, u32[]{:S(2)}) %collective-permute-start.3) | collective-permute-done | bytes 1048608 | tf_op jit(solution)/shard_map/ppermute | solution.py:43
  62.5 2.4 dynamic-slice_dynamic-update-slice_fusion.6
  70.4 10.1 %collective-permute-done.4 = bf16[512,1024]{1,0:T(8,128)(2,1)} collective-permute-done((bf16[512,1024]{1,0:T(8,128)(2,1)S(1)}, bf16[512,1024]{1,0:T(8,128)(2,1)}, u32[]{:S(2)}, u32[]{:S(2)}) %collective-permute-start.4) | collective-permute-done | bytes 1048608 | tf_op jit(solution)/shard_map/ppermute | solution.py:43
  80.6 2.9 collective-permute-start.6
  85.8 2.5 dynamic-slice_dynamic-update-slice_fusion.3
  88.3 2.9 dynamic-slice_dynamic-update-slice_fusion.2
  91.2 2.4 dynamic-slice_dynamic-update-slice_fusion.1
  93.6 2.4 dynamic-slice_dynamic-update-slice_fusion
  96.7 2.9 collective-permute-start.9
  102.6 2.9 collective-permute-start.12
  106.4 2.4 collective-permute-done.6
  110.9 20.3 %collective-permute-done.9 = bf16[512,1024]{1,0:T(8,128)(2,1)S(1)} collective-permute-done((bf16[512,1024]{1,0:T(8,128)(2,1)S(1)}, bf16[512,1024]{1,0:T(8,128)(2,1)S(1)}, u32[]{:S(2)}, u32[]{:S(2)}) %collective-permute-start.9) | collective-permute-done | bytes 1048608 | tf_op jit(solution)/shard_map/ppermute | solution.py:48
  132.1 18.0 %collective-permute-done.12 = bf16[512,1024]{1,0:T(8,128)(2,1)S(1)} collective-permute-done((bf16[512,1024]{1,0:T(8,128)(2,1)S(1)}, bf16[512,1024]{1,0:T(8,128)(2,1)S(1)}, u32[]{:S(2)}, u32[]{:S(2)}) %collective-permute-start.12) | collective-permute-done | bytes 1048608 | tf_op jit(solution)/shard_map/ppermute | solution.py:48
  150.5 7.8 %add_convert_fusion.3 = bf16[512,1024]{1,0:T(8,128)(2,1)} fusion(bf16[4096,1024]{1,0:T(8,128)(2,1)S(1)} %select_dynamic-update-slice_fusion, bf16[1024,4096]{1,0:T(8,128)(2,1)} %dynamic-slice_dynamic-update-slice_fusion, f32[1024]{0:T(1024)S(1)} %copy-done.12), kind=kOutput, calls=%fused_computation.39 | convolution fusion | flops 4296015872 | bytes 13635584 | tf_op jit(solution)/shard_map/dot_general | solution.py:80
  159.1 6.8 %add_convert_fusion.1 = bf16[512,1024]{1,0:T(8,128)(2,1)S(1)} fusion(bf16[4096,1024]{1,0:T(8,128)(2,1)S(1)} %select_dynamic-update-slice_fusion, bf16[1024,4096]{1,0:T(8,128)(2,1)} %dynamic-slice_dynamic-update-slice_fusion, f32[1024]{0:T(1024)S(1)} %copy-done.12), kind=kOutput, calls=%fused_computation.37 | convolution fusion | flops 4296015872 | bytes 13635584 | tf_op jit(solution)/shard_map/dot_general | solution.py:80
  167.8 3.3 fusion.30
  171.1 4.4 fusion.28
  175.5 9.1 %collective-permute-done.14 = bf16[512,1024]{1,0:T(8,128)(2,1)S(1)} collective-permute-done((bf16[512,1024]{1,0:T(8,128)(2,1)}, bf16[512,1024]{1,0:T(8,128)(2,1)S(1)}, u32[]{:S(2)}, u32[]{:S(2)}) %collective-permute-start.14) | collective-permute-done | bytes 1048608 | tf_op jit(solution)/shard_map/ppermute | solution.py:15
  184.6 2.9 fusion.22
  187.5 15.1 %collective-permute-done.18 = bf16[512,1024]{1,0:T(8,128)(2,1)S(1)} collective-permute-done((bf16[512,1024]{1,0:T(8,128)(2,1)S(1)}, bf16[512,1024]{1,0:T(8,128)(2,1)S(1)}, u32[]{:S(2)}, u32[]{:S(2)}) %collective-permute-start.18) | collective-permute-done | bytes 1048608 | tf_op jit(solution)/shard_map/ppermute | solution.py:15
  202.6 3.0 fusion.20
  206.9 2.6 fusion.24
  213.1 5.3 %fusion.5 = (f32[1024]{0:T(1024)S(1)}, f32[1024]{0:T(1024)S(1)}, bf16[512,1024]{1,0:T(8,128)(2,1)S(1)}) fusion(bf16[512,1024]{1,0:T(8,128)(2,1)} %collective-permute-done.19, bf16[1024,4096]{1,0:T(8,128)(2,1)} %param.6, s32[]{:T(128)S(6)} %select_n.225, f32[512,1024]{1,0:T(8,128)} %fusion.20, f32[512,1024]{1,0:T(8,128)} %fusion.28, f32[512,1024]{1,0:T(8,128)} %fusion.24), kind=kOutput, calls=%fused_computation.14 | convolution fusion | flops 1077934080 | bytes 10493956 | tf_op jit(solution)/shard_map/dot_general | solution.py:23
  221.7 2.4 constant_dynamic-slice_fusion.20
  231.8 7.4 %collective-permute-done.31 = bf16[512,512]{1,0:T(8,128)(2,1)} collective-permute-done((bf16[512,512]{1,0:T(8,128)(2,1)S(1)}, bf16[512,512]{1,0:T(8,128)(2,1)}, u32[]{:S(2)}, u32[]{:S(2)}) %collective-permute-start.31) | collective-permute-done | bytes 524320 | tf_op jit(solution)/shard_map/ppermute | solution.py:15
  239.2 3.1 fusion.63
  242.3 7.1 %collective-permute-done.33 = bf16[512,512]{1,0:T(8,128)(2,1)} collective-permute-done((bf16[512,512]{1,0:T(8,128)(2,1)S(1)}, bf16[512,512]{1,0:T(8,128)(2,1)}, u32[]{:S(2)}, u32[]{:S(2)}) %collective-permute-start.33) | collective-permute-done | bytes 524320 | tf_op jit(solution)/shard_map/ppermute | solution.py:15
  249.4 3.1 fusion.65
  263.5 2.4 collective-permute-start.23
  270.9 2.6 reshape.146
  273.5 3.2 fusion.57
  281.8 3.1 fusion.67
  285.0 18.6 %collective-permute-done.25 = f32[4,1152]{1,0:T(4,128)S(1)} collective-permute-done((f32[4,1152]{1,0:T(4,128)S(1)}, f32[4,1152]{1,0:T(4,128)S(1)}, u32[]{:S(2)}, u32[]{:S(2)}) %collective-permute-start.25) | collective-permute-done | bytes 18464 | tf_op jit(solution)/shard_map/ppermute | solution.py:15
  303.6 3.1 fusion.69
  308.7 5.6 %multiply_bitcast_fusion.3 = f32[1,512,1024]{2,1,0:T(8,128)} fusion(f32[512,1024]{1,0:T(8,128)} %fusion.58, f32[512,1024]{1,0:T(8,128)} %fusion.56, f32[512,1024]{1,0:T(8,128)} %fusion.57, bf16[512,512]{1,0:T(8,128)(2,1)} %bitcast.106, bf16[512,1024]{1,0:T(8,128)(2,1)} %collective-permute-done.20, f32[]{:T(128)S(6)} %exp2.7, ...), kind=kOutput, calls=%fused_computation.35 | convolution fusion | flops 540016640 | bytes 9967620 | tf_op jit(solution)/shard_map/dot_general | solution.py:19
  325.9 6.0 %multiply_bitcast_fusion.2 = (f32[1,512,1024]{2,1,0:T(8,128)S(1)}, f32[1,512,1024]{2,1,0:T(8,128)}, f32[1,512,1024]{2,1,0:T(8,128)}) fusion(f32[512,1024]{1,0:T(8,128)S(1)} %fusion.62, f32[512,1024]{1,0:T(8,128)S(1)} %copy-done.4, f32[512,1024]{1,0:T(8,128)S(1)} %copy-done.3, f32[512,1024]{1,0:T(8,128)S(1)} %fusion.60, f32[512]{0:T(512)S(1)} %bitcast.139, ...), kind=kOutput, calls=%fused_computation.34 | convolution fusion | flops 546308096 | bytes 30943236 | tf_op jit(solution)/shard_map/dot_general | solution.py:19
  332.0 3.2 pad_maximum_fusion
  335.2 3.3 copy-done
  340.8 2.5 collective-permute-start.42
  346.9 19.3 %collective-permute-done.42 = f16[512,1024]{1,0:T(8,128)(2,1)S(1)} collective-permute-done((f16[512,1024]{1,0:T(8,128)(2,1)}, f16[512,1024]{1,0:T(8,128)(2,1)S(1)}, u32[]{:S(2)}, u32[]{:S(2)}) %collective-permute-start.42) | collective-permute-done | bytes 1048608 | tf_op jit(solution)/shard_map/ppermute | solution.py:151
  366.2 3.3 fusion.11
  369.5 31.4 %collective-permute-start.43 = (f16[512,1024]{1,0:T(8,128)(2,1)S(1)}, f16[512,1024]{1,0:T(8,128)(2,1)S(1)}, u32[]{:S(2)}, u32[]{:S(2)}) collective-permute-start(f16[512,1024]{1,0:T(8,128)(2,1)S(1)} %get-tuple-element.13), channel_id=1, source_target_pairs={{0,8},{4,12},{8,16},{12,20},{1,9},{5,13},{9,17},{13,21},{2,10},{6,... | collective-permute-start | bytes 3145736 | tf_op jit(solution)/shard_map/ppermute | solution.py:151
  402.2 19.7 %collective-permute-done.43 = f16[512,1024]{1,0:T(8,128)(2,1)S(1)} collective-permute-done((f16[512,1024]{1,0:T(8,128)(2,1)S(1)}, f16[512,1024]{1,0:T(8,128)(2,1)S(1)}, u32[]{:S(2)}, u32[]{:S(2)}) %collective-permute-start.43) | collective-permute-done | bytes 1048608 | tf_op jit(solution)/shard_map/ppermute | solution.py:151
  423.9 4.5 collective-permute-start.44
  428.5 20.0 %collective-permute-done.44 = f16[512,1024]{1,0:T(8,128)(2,1)S(1)} collective-permute-done((f16[512,1024]{1,0:T(8,128)(2,1)S(1)}, f16[512,1024]{1,0:T(8,128)(2,1)S(1)}, u32[]{:S(2)}, u32[]{:S(2)}) %collective-permute-start.44) | collective-permute-done | bytes 1048608 | tf_op jit(solution)/shard_map/ppermute | solution.py:151
  448.5 3.6 fusion.15
  (158 shorter events, 87.9 us)
Async XLA Ops:
  0.6 28.3 %collective-permute-start.2 = (bf16[512,1024]{1,0:T(8,128)(2,1)}, bf16[512,1024]{1,0:T(8,128)(2,1)S(1)}, u32[]{:S(2)}, u32[]{:S(2)}) collective-permute-start(bf16[512,1024]{1,0:T(8,128)(2,1)} %param.5), channel_id=1, source_target_pairs={{8,0},{12,4},{16,8},{20,12},{24,16},{28,20},{9,1},{13,5},{17,9},{2... | collective-permute-start | bytes 3145736 | tf_op jit(solution)/shard_map/ppermute | solution.py:43
  1.9 28.3 %collective-permute-start.1 = (bf16[512,1024]{1,0:T(8,128)(2,1)}, bf16[512,1024]{1,0:T(8,128)(2,1)}, u32[]{:S(2)}, u32[]{:S(2)}) collective-permute-start(bf16[512,1024]{1,0:T(8,128)(2,1)} %param.5), channel_id=1, source_target_pairs={{0,8},{4,12},{8,16},{12,20},{16,24},{20,28},{1,9},{5,13},{9,17},{1... | collective-permute-start | bytes 3145736 | tf_op jit(solution)/shard_map/ppermute | solution.py:43
  28.9 26.2 %collective-permute-start.3 = (bf16[512,1024]{1,0:T(8,128)(2,1)S(1)}, bf16[512,1024]{1,0:T(8,128)(2,1)S(1)}, u32[]{:S(2)}, u32[]{:S(2)}) collective-permute-start(bf16[512,1024]{1,0:T(8,128)(2,1)S(1)} %collective-permute-done.2), channel_id=1, source_target_pairs={{8,0},{12,4},{16,8},{20,12},{9,1},{13,5},{17,9},{21,13},{10,2},{14... | collective-permute-start | bytes 3145736 | tf_op jit(solution)/shard_map/ppermute | solution.py:43
  30.2 38.6 %collective-permute-start.7 = (bf16[512,1024]{1,0:T(8,128)(2,1)}, bf16[512,1024]{1,0:T(8,128)(2,1)S(1)}, u32[]{:S(2)}, u32[]{:S(2)}) collective-permute-start(bf16[512,1024]{1,0:T(8,128)(2,1)} %collective-permute-done.1), channel_id=1, source_target_pairs={{8,16},{12,20},{16,24},{20,28},{9,17},{13,21},{17,25},{21,29},{10,... | collective-permute-start | bytes 3145736 | tf_op jit(solution)/shard_map/ppermute | solution.py:43
  55.2 25.4 %collective-permute-start.4 = (bf16[512,1024]{1,0:T(8,128)(2,1)S(1)}, bf16[512,1024]{1,0:T(8,128)(2,1)}, u32[]{:S(2)}, u32[]{:S(2)}) collective-permute-start(bf16[512,1024]{1,0:T(8,128)(2,1)S(1)} %collective-permute-done.3), channel_id=1, source_target_pairs={{8,0},{12,4},{9,1},{13,5},{10,2},{14,6},{11,3},{15,7}} | collective-permute-start | bytes 3145736 | tf_op jit(solution)/shard_map/ppermute | solution.py:43
  56.4 40.2 %collective-permute-start = (bf16[512,1024]{1,0:T(8,128)(2,1)}, bf16[512,1024]{1,0:T(8,128)(2,1)}, u32[]{:S(2)}, u32[]{:S(2)}) collective-permute-start(bf16[512,1024]{1,0:T(8,128)(2,1)} %param.5), channel_id=1, source_target_pairs={{0,4},{4,0},{8,12},{12,8},{16,20},{20,16},{24,28},{28,24},{1,5},{5... | collective-permute-start | bytes 3145736 | tf_op jit(solution)/shard_map/ppermute | solution.py:15
  67.1 35.4 %collective-permute-start.5 = (bf16[512,1024]{1,0:T(8,128)(2,1)}, bf16[512,1024]{1,0:T(8,128)(2,1)}, u32[]{:S(2)}, u32[]{:S(2)}) collective-permute-start(bf16[512,1024]{1,0:T(8,128)(2,1)} %collective-permute-done.1), channel_id=1, source_target_pairs={{8,12},{12,8},{16,20},{20,16},{24,28},{28,24},{9,13},{13,9},{17,21... | collective-permute-start | bytes 3145736 | tf_op jit(solution)/shard_map/ppermute | solution.py:48
  68.8 36.7 %collective-permute-start.10 = (bf16[512,1024]{1,0:T(8,128)(2,1)S(1)}, bf16[512,1024]{1,0:T(8,128)(2,1)}, u32[]{:S(2)}, u32[]{:S(2)}) collective-permute-start(bf16[512,1024]{1,0:T(8,128)(2,1)S(1)} %collective-permute-done.7), channel_id=1, source_target_pairs={{16,24},{20,28},{17,25},{21,29},{18,26},{22,30},{19,27},{23,31}} | collective-permute-start | bytes 3145736 | tf_op jit(solution)/shard_map/ppermute | solution.py:43
  80.6 28.3 %collective-permute-start.6 = (bf16[512,1024]{1,0:T(8,128)(2,1)}, bf16[512,1024]{1,0:T(8,128)(2,1)}, u32[]{:S(2)}, u32[]{:S(2)}) collective-permute-start(bf16[512,1024]{1,0:T(8,128)(2,1)} %collective-permute-done.4), channel_id=1, source_target_pairs={{0,4},{4,0},{1,5},{5,1},{2,6},{6,2},{3,7},{7,3}} | collective-permute-start | bytes 3145736 | tf_op jit(solution)/shard_map/ppermute | solution.py:48
  96.0 14.9 %collective-permute-start.8 = (bf16[512,1024]{1,0:T(8,128)(2,1)S(1)}, bf16[512,1024]{1,0:T(8,128)(2,1)S(1)}, u32[]{:S(2)}, u32[]{:S(2)}) collective-permute-start(bf16[512,1024]{1,0:T(8,128)(2,1)S(1)} %collective-permute-done.7), channel_id=1, source_target_pairs={{16,20},{20,16},{24,28},{28,24},{17,21},{21,17},{25,29},{29,25},{1... | collective-permute-start | bytes 3145736 | tf_op jit(solution)/shard_map/ppermute | solution.py:48
  96.7 34.5 %collective-permute-start.9 = (bf16[512,1024]{1,0:T(8,128)(2,1)S(1)}, bf16[512,1024]{1,0:T(8,128)(2,1)S(1)}, u32[]{:S(2)}, u32[]{:S(2)}) collective-permute-start(bf16[512,1024]{1,0:T(8,128)(2,1)S(1)} %collective-permute-done.3), channel_id=1, source_target_pairs={{0,4},{4,0},{8,12},{12,8},{1,5},{5,1},{9,13},{13,9},{2,6},{6,2},{1... | collective-permute-start | bytes 3145736 | tf_op jit(solution)/shard_map/ppermute | solution.py:48
  102.6 47.5 %collective-permute-start.12 = (bf16[512,1024]{1,0:T(8,128)(2,1)S(1)}, bf16[512,1024]{1,0:T(8,128)(2,1)S(1)}, u32[]{:S(2)}, u32[]{:S(2)}) collective-permute-start(bf16[512,1024]{1,0:T(8,128)(2,1)S(1)} %collective-permute-done.2), channel_id=1, source_target_pairs={{0,4},{4,0},{8,12},{12,8},{16,20},{20,16},{1,5},{5,1},{9,13},{13,9... | collective-permute-start | bytes 3145736 | tf_op jit(solution)/shard_map/ppermute | solution.py:48
  105.5 44.6 %collective-permute-start.11 = (bf16[512,1024]{1,0:T(8,128)(2,1)}, bf16[512,1024]{1,0:T(8,128)(2,1)S(1)}, u32[]{:S(2)}, u32[]{:S(2)}) collective-permute-start(bf16[512,1024]{1,0:T(8,128)(2,1)} %collective-permute-done.10), channel_id=1, source_target_pairs={{24,28},{28,24},{25,29},{29,25},{26,30},{30,26},{27,31},{31,27}} | collective-permute-start | bytes 3145736 | tf_op jit(solution)/shard_map/ppermute | solution.py:48
  158.3 26.3 %collective-permute-start.14 = (bf16[512,1024]{1,0:T(8,128)(2,1)}, bf16[512,1024]{1,0:T(8,128)(2,1)S(1)}, u32[]{:S(2)}, u32[]{:S(2)}) collective-permute-start(bf16[512,1024]{1,0:T(8,128)(2,1)} %add_convert_fusion.3), channel_id=1, source_target_pairs={{0,2},{1,3},{2,0},{3,1},{4,6},{5,7},{6,4},{7,5},{8,10},{9,11},{10,... | collective-permute-start | bytes 3145736 | tf_op jit(solution)/shard_map/ppermute | solution.py:15
  165.9 36.7 %collective-permute-start.18 = (bf16[512,1024]{1,0:T(8,128)(2,1)S(1)}, bf16[512,1024]{1,0:T(8,128)(2,1)S(1)}, u32[]{:S(2)}, u32[]{:S(2)}) collective-permute-start(bf16[512,1024]{1,0:T(8,128)(2,1)S(1)} %add_convert_fusion.1), channel_id=1, source_target_pairs={{0,2},{1,3},{2,0},{3,1},{4,6},{5,7},{6,4},{7,5},{8,10},{9,11},{10,... | collective-permute-start | bytes 3145736 | tf_op jit(solution)/shard_map/ppermute | solution.py:15
  167.3 38.4 %collective-permute-start.13 = (bf16[512,1024]{1,0:T(8,128)(2,1)}, bf16[512,1024]{1,0:T(8,128)(2,1)S(1)}, u32[]{:S(2)}, u32[]{:S(2)}) collective-permute-start(bf16[512,1024]{1,0:T(8,128)(2,1)} %add_convert_fusion.3), channel_id=1, source_target_pairs={{0,1},{1,0},{2,3},{3,2},{4,5},{5,4},{6,7},{7,6},{8,9},{9,8},{10,11... | collective-permute-start | bytes 3145736 | tf_op jit(solution)/shard_map/ppermute | solution.py:15
  167.3 39.7 %collective-permute-start.17 = (bf16[512,1024]{1,0:T(8,128)(2,1)S(1)}, bf16[512,1024]{1,0:T(8,128)(2,1)S(1)}, u32[]{:S(2)}, u32[]{:S(2)}) collective-permute-start(bf16[512,1024]{1,0:T(8,128)(2,1)S(1)} %add_convert_fusion.1), channel_id=1, source_target_pairs={{0,1},{1,0},{2,3},{3,2},{4,5},{5,4},{6,7},{7,6},{8,9},{9,8},{10,11... | collective-permute-start | bytes 3145736 | tf_op jit(solution)/shard_map/ppermute | solution.py:15
  167.8 34.8 %slice-start = ((s8[8388608]{0:T(1024)(128)(4,1)}), s8[4194304]{0:T(1024)(128)(4,1)S(1)}, s32[]{:S(2)}) async-start(s8[8388608]{0:T(1024)(128)(4,1)} %bitcast.116), calls=%async_computation | async-start | bytes 8388608
  171.1 31.5 %slice-start.1 = ((s8[8388608]{0:T(1024)(128)(4,1)}), s8[4194304]{0:T(1024)(128)(4,1)S(1)}, s32[]{:S(2)}) async-start(s8[8388608]{0:T(1024)(128)(4,1)} %bitcast.116), calls=%async_computation.1 | async-start | bytes 8388608
  184.6 24.9 %collective-permute-start.15 = (bf16[512,1024]{1,0:T(8,128)(2,1)S(1)}, bf16[512,1024]{1,0:T(8,128)(2,1)S(1)}, u32[]{:S(2)}, u32[]{:S(2)}) collective-permute-start(bf16[512,1024]{1,0:T(8,128)(2,1)S(1)} %collective-permute-done.14), channel_id=1, source_target_pairs={{0,1},{1,0},{2,3},{3,2},{4,5},{5,4},{6,7},{7,6},{8,9},{9,8},{10,11... | collective-permute-start | bytes 3145736 | tf_op jit(solution)/shard_map/ppermute | solution.py:15
  202.6 10.5 %collective-permute-start.19 = (bf16[512,1024]{1,0:T(8,128)(2,1)S(1)}, bf16[512,1024]{1,0:T(8,128)(2,1)}, u32[]{:S(2)}, u32[]{:S(2)}) collective-permute-start(bf16[512,1024]{1,0:T(8,128)(2,1)S(1)} %collective-permute-done.18), channel_id=1, source_target_pairs={{0,1},{1,0},{2,3},{3,2},{4,5},{5,4},{6,7},{7,6},{8,9},{9,8},{10,11... | collective-permute-start | bytes 3145736 | tf_op jit(solution)/shard_map/ppermute | solution.py:15
  211.1 46.1 %collective-permute-start.16 = (bf16[512,1024]{1,0:T(8,128)(2,1)S(1)}, bf16[512,1024]{1,0:T(8,128)(2,1)S(1)}, u32[]{:S(2)}, u32[]{:S(2)}) collective-permute-start(bf16[512,1024]{1,0:T(8,128)(2,1)S(1)} %get-tuple-element.37), channel_id=1, source_target_pairs={{0,4},{4,0},{8,12},{12,8},{16,20},{20,16},{24,28},{28,24},{1,5},{5... | collective-permute-start | bytes 3145736 | tf_op jit(solution)/shard_map/ppermute | solution.py:15
  218.4 40.9 %collective-permute-start.20 = (bf16[512,1024]{1,0:T(8,128)(2,1)S(1)}, bf16[512,1024]{1,0:T(8,128)(2,1)}, u32[]{:S(2)}, u32[]{:S(2)}) collective-permute-start(bf16[512,1024]{1,0:T(8,128)(2,1)S(1)} %get-tuple-element.38), channel_id=1, source_target_pairs={{0,4},{4,0},{8,12},{12,8},{16,20},{20,16},{24,28},{28,24},{1,5},{5... | collective-permute-start | bytes 3145736 | tf_op jit(solution)/shard_map/ppermute | solution.py:15
  224.2 15.0 %collective-permute-start.31 = (bf16[512,512]{1,0:T(8,128)(2,1)S(1)}, bf16[512,512]{1,0:T(8,128)(2,1)}, u32[]{:S(2)}, u32[]{:S(2)}) collective-permute-start(bf16[512,512]{1,0:T(8,128)(2,1)S(1)} %bitcast.110), channel_id=1, source_target_pairs={{0,2},{1,3},{2,0},{3,1},{4,6},{5,7},{6,4},{7,5},{8,10},{9,11},{10,... | collective-permute-start | bytes 1572872 | tf_op jit(solution)/shard_map/ppermute | solution.py:15
  224.7 27.8 %collective-permute-start.27 = (bf16[512,512]{1,0:T(8,128)(2,1)S(1)}, bf16[512,512]{1,0:T(8,128)(2,1)S(1)}, u32[]{:S(2)}, u32[]{:S(2)}) collective-permute-start(bf16[512,512]{1,0:T(8,128)(2,1)S(1)} %bitcast.111), channel_id=1, source_target_pairs={{0,1},{1,0},{2,3},{3,2},{4,5},{5,4},{6,7},{7,6},{8,9},{9,8},{10,11... | collective-permute-start | bytes 1572872 | tf_op jit(solution)/shard_map/ppermute | solution.py:15
  225.9 23.5 %collective-permute-start.33 = (bf16[512,512]{1,0:T(8,128)(2,1)S(1)}, bf16[512,512]{1,0:T(8,128)(2,1)}, u32[]{:S(2)}, u32[]{:S(2)}) collective-permute-start(bf16[512,512]{1,0:T(8,128)(2,1)S(1)} %bitcast.113), channel_id=1, source_target_pairs={{0,2},{1,3},{2,0},{3,1},{4,6},{5,7},{6,4},{7,5},{8,10},{9,11},{10,... | collective-permute-start | bytes 1572872 | tf_op jit(solution)/shard_map/ppermute | solution.py:15
  239.2 15.9 %collective-permute-start.29 = (bf16[512,512]{1,0:T(8,128)(2,1)S(1)}, bf16[512,512]{1,0:T(8,128)(2,1)S(1)}, u32[]{:S(2)}, u32[]{:S(2)}) collective-permute-start(bf16[512,512]{1,0:T(8,128)(2,1)S(1)} %bitcast.115), channel_id=1, source_target_pairs={{0,1},{1,0},{2,3},{3,2},{4,5},{5,4},{6,7},{7,6},{8,9},{9,8},{10,11... | collective-permute-start | bytes 1572872 | tf_op jit(solution)/shard_map/ppermute | solution.py:15
  249.4 31.7 %collective-permute-start.35 = (bf16[512,512]{1,0:T(8,128)(2,1)}, bf16[512,512]{1,0:T(8,128)(2,1)}, u32[]{:S(2)}, u32[]{:S(2)}) collective-permute-start(bf16[512,512]{1,0:T(8,128)(2,1)} %collective-permute-done.31), channel_id=1, source_target_pairs={{0,1},{1,0},{2,3},{3,2},{4,5},{5,4},{6,7},{7,6},{8,9},{9,8},{10,11... | collective-permute-start | bytes 1572872 | tf_op jit(solution)/shard_map/ppermute | solution.py:15
  252.5 32.5 %collective-permute-start.37 = (bf16[512,512]{1,0:T(8,128)(2,1)}, bf16[512,512]{1,0:T(8,128)(2,1)}, u32[]{:S(2)}, u32[]{:S(2)}) collective-permute-start(bf16[512,512]{1,0:T(8,128)(2,1)} %collective-permute-done.33), channel_id=1, source_target_pairs={{0,1},{1,0},{2,3},{3,2},{4,5},{5,4},{6,7},{7,6},{8,9},{9,8},{10,11... | collective-permute-start | bytes 1572872 | tf_op jit(solution)/shard_map/ppermute | solution.py:15
  262.1 16.7 %collective-permute-start.21 = (f32[1152]{0:T(1024)S(1)}, f32[1152]{0:T(1024)S(1)}, u32[]{:S(2)}, u32[]{:S(2)}) collective-permute-start(f32[1152]{0:T(1024)S(1)} %concatenate.11), channel_id=1, source_target_pairs={{0,8},{4,12},{8,16},{12,20},{16,24},{20,28},{24,0},{28,4},{1,9},{5... | collective-permute-start | bytes 13832 | tf_op jit(solution)/shard_map/ppermute | solution.py:103
  263.5 15.9 %collective-permute-start.22 = (f32[1152]{0:T(1024)S(1)}, f32[1152]{0:T(1024)S(1)}, u32[]{:S(2)}, u32[]{:S(2)}) collective-permute-start(f32[1152]{0:T(1024)S(1)} %concatenate.11), channel_id=1, source_target_pairs={{0,16},{4,20},{8,24},{12,28},{16,0},{20,4},{24,8},{28,12},{1,17},{... | collective-permute-start | bytes 13832 | tf_op jit(solution)/shard_map/ppermute | solution.py:103
  263.5 16.0 %collective-permute-start.23 = (f32[1152]{0:T(1024)S(1)}, f32[1152]{0:T(1024)S(1)}, u32[]{:S(2)}, u32[]{:S(2)}) collective-permute-start(f32[1152]{0:T(1024)S(1)} %concatenate.11), channel_id=1, source_target_pairs={{0,24},{4,28},{8,0},{12,4},{16,8},{20,12},{24,16},{28,20},{1,25},{... | collective-permute-start | bytes 13832 | tf_op jit(solution)/shard_map/ppermute | solution.py:103
  278.7 35.5 %collective-permute-start.32 = (bf16[512,512]{1,0:T(8,128)(2,1)}, bf16[512,512]{1,0:T(8,128)(2,1)}, u32[]{:S(2)}, u32[]{:S(2)}) collective-permute-start(bf16[512,512]{1,0:T(8,128)(2,1)} %bitcast.108), channel_id=1, source_target_pairs={{0,2},{1,3},{2,0},{3,1},{4,6},{5,7},{6,4},{7,5},{8,10},{9,11},{10,... | collective-permute-start | bytes 1572872 | tf_op jit(solution)/shard_map/ppermute | solution.py:15
  279.5 39.4 %collective-permute-start.28 = (bf16[512,512]{1,0:T(8,128)(2,1)}, bf16[512,512]{1,0:T(8,128)(2,1)}, u32[]{:S(2)}, u32[]{:S(2)}) collective-permute-start(bf16[512,512]{1,0:T(8,128)(2,1)} %bitcast.108), channel_id=1, source_target_pairs={{0,1},{1,0},{2,3},{3,2},{4,5},{5,4},{6,7},{7,6},{8,9},{9,8},{10,11... | collective-permute-start | bytes 1572872 | tf_op jit(solution)/shard_map/ppermute | solution.py:15
  279.6 34.7 %collective-permute-start.34 = (bf16[512,512]{1,0:T(8,128)(2,1)}, bf16[512,512]{1,0:T(8,128)(2,1)}, u32[]{:S(2)}, u32[]{:S(2)}) collective-permute-start(bf16[512,512]{1,0:T(8,128)(2,1)} %bitcast.106), channel_id=1, source_target_pairs={{0,2},{1,3},{2,0},{3,1},{4,6},{5,7},{6,4},{7,5},{8,10},{9,11},{10,... | collective-permute-start | bytes 1572872 | tf_op jit(solution)/shard_map/ppermute | solution.py:15
  281.0 22.5 %collective-permute-start.25 = (f32[4,1152]{1,0:T(4,128)S(1)}, f32[4,1152]{1,0:T(4,128)S(1)}, u32[]{:S(2)}, u32[]{:S(2)}) collective-permute-start(f32[4,1152]{1,0:T(4,128)S(1)} %get-tuple-element.29), channel_id=1, source_target_pairs={{0,2},{1,3},{2,0},{3,1},{4,6},{5,7},{6,4},{7,5},{8,10},{9,11},{10,... | collective-permute-start | bytes 55304 | tf_op jit(solution)/shard_map/ppermute | solution.py:15
  285.0 21.7 %collective-permute-start.24 = (f32[4,1152]{1,0:T(4,128)S(1)}, f32[4,1152]{1,0:T(4,128)S(1)}, u32[]{:S(2)}, u32[]{:S(2)}) collective-permute-start(f32[4,1152]{1,0:T(4,128)S(1)} %get-tuple-element.29), channel_id=1, source_target_pairs={{0,1},{1,0},{2,3},{3,2},{4,5},{5,4},{6,7},{7,6},{8,9},{9,8},{10,11... | collective-permute-start | bytes 55304 | tf_op jit(solution)/shard_map/ppermute | solution.py:15
  303.6 3.6 collective-permute-start.26
  306.6 14.1 %collective-permute-start.30 = (bf16[512,512]{1,0:T(8,128)(2,1)}, bf16[512,512]{1,0:T(8,128)(2,1)S(1)}, u32[]{:S(2)}, u32[]{:S(2)}) collective-permute-start(bf16[512,512]{1,0:T(8,128)(2,1)} %bitcast.106), channel_id=1, source_target_pairs={{0,1},{1,0},{2,3},{3,2},{4,5},{5,4},{6,7},{7,6},{8,9},{9,8},{10,11... | collective-permute-start | bytes 1572872 | tf_op jit(solution)/shard_map/ppermute | solution.py:15
  314.2 8.7 %collective-permute-start.36 = (bf16[512,512]{1,0:T(8,128)(2,1)}, bf16[512,512]{1,0:T(8,128)(2,1)S(1)}, u32[]{:S(2)}, u32[]{:S(2)}) collective-permute-start(bf16[512,512]{1,0:T(8,128)(2,1)} %collective-permute-done.32), channel_id=1, source_target_pairs={{0,1},{1,0},{2,3},{3,2},{4,5},{5,4},{6,7},{7,6},{8,9},{9,8},{10,11... | collective-permute-start | bytes 1572872 | tf_op jit(solution)/shard_map/ppermute | solution.py:15
  314.3 10.8 %collective-permute-start.38 = (bf16[512,512]{1,0:T(8,128)(2,1)}, bf16[512,512]{1,0:T(8,128)(2,1)S(1)}, u32[]{:S(2)}, u32[]{:S(2)}) collective-permute-start(bf16[512,512]{1,0:T(8,128)(2,1)} %collective-permute-done.34), channel_id=1, source_target_pairs={{0,1},{1,0},{2,3},{3,2},{4,5},{5,4},{6,7},{7,6},{8,9},{9,8},{10,11... | collective-permute-start | bytes 1572872 | tf_op jit(solution)/shard_map/ppermute | solution.py:15
  339.8 3.5 collective-permute-start.39
  340.8 25.4 %collective-permute-start.42 = (f16[512,1024]{1,0:T(8,128)(2,1)}, f16[512,1024]{1,0:T(8,128)(2,1)S(1)}, u32[]{:S(2)}, u32[]{:S(2)}) collective-permute-start(f16[512,1024]{1,0:T(8,128)(2,1)} %get-tuple-element.15), channel_id=1, source_target_pairs={{0,8},{4,12},{1,9},{5,13},{2,10},{6,14},{3,11},{7,15}} | collective-permute-start | bytes 3145736 | tf_op jit(solution)/shard_map/ppermute | solution.py:151
  345.3 20.9 %collective-permute-start.40 = (f16[512,1024]{1,0:T(8,128)(2,1)S(1)}, f16[512,1024]{1,0:T(8,128)(2,1)}, u32[]{:S(2)}, u32[]{:S(2)}) collective-permute-start(f16[512,1024]{1,0:T(8,128)(2,1)S(1)} %fusion.10), channel_id=1, source_target_pairs={{24,16},{28,20},{16,8},{20,12},{25,17},{29,21},{17,9},{21,13},{26,... | collective-permute-start | bytes 3145736 | tf_op jit(solution)/shard_map/ppermute | solution.py:151
  369.5 52.5 %collective-permute-start.43 = (f16[512,1024]{1,0:T(8,128)(2,1)S(1)}, f16[512,1024]{1,0:T(8,128)(2,1)S(1)}, u32[]{:S(2)}, u32[]{:S(2)}) collective-permute-start(f16[512,1024]{1,0:T(8,128)(2,1)S(1)} %get-tuple-element.13), channel_id=1, source_target_pairs={{0,8},{4,12},{8,16},{12,20},{1,9},{5,13},{9,17},{13,21},{2,10},{6,... | collective-permute-start | bytes 3145736 | tf_op jit(solution)/shard_map/ppermute | solution.py:151
  400.9 27.6 %collective-permute-start.41 = (f16[512,1024]{1,0:T(8,128)(2,1)S(1)}, f16[512,1024]{1,0:T(8,128)(2,1)S(1)}, u32[]{:S(2)}, u32[]{:S(2)}) collective-permute-start(f16[512,1024]{1,0:T(8,128)(2,1)S(1)} %get-tuple-element.12), channel_id=1, source_target_pairs={{24,16},{28,20},{16,8},{20,12},{8,0},{12,4},{25,17},{29,21},{17,9}... | collective-permute-start | bytes 3145736 | tf_op jit(solution)/shard_map/ppermute | solution.py:151
  423.9 24.6 %collective-permute-start.44 = (f16[512,1024]{1,0:T(8,128)(2,1)S(1)}, f16[512,1024]{1,0:T(8,128)(2,1)S(1)}, u32[]{:S(2)}, u32[]{:S(2)}) collective-permute-start(f16[512,1024]{1,0:T(8,128)(2,1)S(1)} %fusion.9), channel_id=1, source_target_pairs={{0,8},{4,12},{8,16},{12,20},{16,24},{20,28},{1,9},{5,13},{9,17},{1... | collective-permute-start | bytes 3145736 | tf_op jit(solution)/shard_map/ppermute | solution.py:151
  428.4 23.7 %copy-start.11 = (f32[1024]{0:T(1024)}, f32[1024]{0:T(1024)S(1)}, u32[]{:S(2)}) copy-start(f32[1024]{0:T(1024)S(1)} %broadcast_multiply_fusion) | copy-start | bytes 12292
  (12 other events, 79.3 us)
where the time goes:
time: 457 us; the launch traced here: 452 us
  waiting for transfers between devices  214 us (47%)
  matrix products  84.7 us (19%)
  starting transfers between devices  83.7 us (18%)
  local copies, waits for them, and re-layouts  44.5 us (10%)
  other arithmetic  23.4 us (5%)
    ppermute x24, waiting for transfers between devices, swap(): return lax.ppermute(value, axis, flip(lax.axis_size(axis), bit))  59.1 us
    ppermute x6, waiting for transfers between devices, on_device(): arrived[up] = lax.ppermute(value.astype(F16), 'scen', pairs)  59 us
    ppermute x6, waiting for transfers between devices, along_z(): lax.ppermute(value, 'scen', [(2 * a + x, 2 * b + x) for a, b in pairs for...  54.8 us
    dot_general x16, matrix products, rows_dot(): lax.dot_general(a, b, (((0,), (0,)), ((), ())), preferred_element_type=F32)  45.7 us
    ppermute x6, starting transfers between devices, on_device(): arrived[up] = lax.ppermute(value.astype(F16), 'scen', pairs)  42.3 us
    ppermute x6, waiting for transfers between devices, across_x(): lax.ppermute(value, 'scen', [(2 * z + x, 2 * z + 1 - x) for z in zs for x...  40.8 us
    unnamed x43, local copies, waits for them, and re-layouts  27 us
    dot_general x8, matrix products, cols_dot(): lax.dot_general(a, b, (((1,), (1,)), ((), ())), preferred_element_type=F32)  24.3 us
  transfers between devices with their start and end apart: 45, of which 15 were waited for; matrix products, arithmetic and copies ran while one was open for 27% of the time, Pallas kernels for 0%

commit v1 on v0

--- a/solution.py
+++ b/solution.py
@@ -4,7 +4,7 @@
 from jax.sharding import PartitionSpec as P
 
 BF16, F16, F32 = jnp.bfloat16, jnp.float16, jnp.float32
-CHUNKS = 2
+CHUNKS = 4
 
 
 def flip(size, bit):

time: 457 us -> 495 us (1.083)
  matrix products: 84.7 us -> 106 us
  starting transfers between devices: 83.7 us -> 93.4 us
  local copies, waits for them, and re-layouts: 44.5 us -> 53.1 us
    dot_general x16 -> x32, matrix products: 45.7 us -> 67.1 us  [rows_dot(): lax.dot_general(a, b, (((0,), (0,)), ((), ())), preferred_element_type=F32)]
    ppermute x24 -> x44, starting transfers between devices: 12.8 us -> 21.9 us  [swap(): return lax.ppermute(value, axis, flip(lax.axis_size(axis), bit))]
    reshape x4 -> x8, local copies, waits for them, and re-layouts: 7.48 us -> 11.5 us  [own_parity(): split = value.reshape(value.shape[0], per_fac, 2, block)]
    unnamed x43 -> x59, local copies, waits for them, and re-layouts: 27 us -> 28.6 us
    dot_general x8 -> x16, matrix products: 24.3 us -> 22.9 us  [cols_dot(): lax.dot_general(a, b, (((1,), (1,)), ((), ())), preferred_element_type=F32)]
    ppermute x24 -> x44, waiting for transfers between devices: 59.1 us -> 60.5 us  [swap(): return lax.ppermute(value, axis, flip(lax.axis_size(axis), bit))]
    dot_general x2 -> x4, matrix products: 14.6 us -> 15.9 us  [on_device(): mixed = jnp.dot(draws, lower, preferred_element_type=F32)]
  transfers between devices with their start and end apart: 45 -> 65, of which waited for: 15 -> 20; matrix products, arithmetic and copies ran while one was open for 27% -> 32% of each run, Pallas kernels for 0% -> 0%
where the time goes in v1:
time: 495 us; the launch traced here: 490 us
  waiting for transfers between devices  215 us (43%)
  matrix products  106 us (21%)
  starting transfers between devices  93.4 us (19%)
  local copies, waits for them, and re-layouts  53.1 us (11%)
  other arithmetic  19.7 us (4%)
    dot_general x32, matrix products, rows_dot(): lax.dot_general(a, b, (((0,), (0,)), ((), ())), preferred_element_type=F32)  67.1 us
    ppermute x44, waiting for transfers between devices, swap(): return lax.ppermute(value, axis, flip(lax.axis_size(axis), bit))  60.5 us
    ppermute x6, waiting for transfers between devices, on_device(): arrived[up] = lax.ppermute(value.astype(F16), 'scen', pairs)  59.1 us
    ppermute x6, waiting for transfers between devices, along_z(): lax.ppermute(value, 'scen', [(2 * a + x, 2 * b + x) for a, b in pairs for...  54.8 us
    ppermute x6, starting transfers between devices, on_device(): arrived[up] = lax.ppermute(value.astype(F16), 'scen', pairs)  42.6 us
    ppermute x6, waiting for transfers between devices, across_x(): lax.ppermute(value, 'scen', [(2 * z + x, 2 * z + 1 - x) for z in zs for x...  40.8 us
    unnamed x59, local copies, waits for them, and re-layouts  28.6 us
    dot_general x16, matrix products, cols_dot(): lax.dot_general(a, b, (((1,), (1,)), ((), ())), preferred_element_type=F32)  22.9 us
  transfers between devices with their start and end apart: 65, of which 20 were waited for; matrix products, arithmetic and copies ran while one was open for 32% of the time, Pallas kernels for 0%

profile of v1, /device:TPU:0, one launch (start us, length us, event | category | flops | bytes accessed | tf_op | source)
XLA Modules:
  0.0 490.1 jit_solution(244550682805935927)
XLA Ops:
  1.9 6.6 %collective-permute-start.1 = (bf16[512,1024]{1,0:T(8,128)(2,1)}, bf16[512,1024]{1,0:T(8,128)(2,1)}, u32[]{:S(2)}, u32[]{:S(2)}) collective-permute-start(bf16[512,1024]{1,0:T(8,128)(2,1)} %param.5), channel_id=1, source_target_pairs={{0,8},{4,12},{8,16},{12,20},{16,24},{20,28},{1,9},{5,13},{9,17},{1... | collective-permute-start | bytes 3145736 | tf_op jit(solution)/shard_map/ppermute | solution.py:43
  8.5 20.4 %collective-permute-done.2 = bf16[512,1024]{1,0:T(8,128)(2,1)S(1)} collective-permute-done((bf16[512,1024]{1,0:T(8,128)(2,1)}, bf16[512,1024]{1,0:T(8,128)(2,1)S(1)}, u32[]{:S(2)}, u32[]{:S(2)}) %collective-permute-start.2) | collective-permute-done | bytes 1048608 | tf_op jit(solution)/shard_map/ppermute | solution.py:43
  31.0 24.2 %collective-permute-done.3 = bf16[512,1024]{1,0:T(8,128)(2,1)S(1)} collective-permute-done((bf16[512,1024]{1,0:T(8,128)(2,1)S(1)}, bf16[512,1024]{1,0:T(8,128)(2,1)S(1)}, u32[]{:S(2)}, u32[]{:S(2)}) %collective-permute-start.3) | collective-permute-done | bytes 1048608 | tf_op jit(solution)/shard_map/ppermute | solution.py:43
  70.4 10.2 %collective-permute-done.4 = bf16[512,1024]{1,0:T(8,128)(2,1)} collective-permute-done((bf16[512,1024]{1,0:T(8,128)(2,1)S(1)}, bf16[512,1024]{1,0:T(8,128)(2,1)}, u32[]{:S(2)}, u32[]{:S(2)}) %collective-permute-start.4) | collective-permute-done | bytes 1048608 | tf_op jit(solution)/shard_map/ppermute | solution.py:43
  80.6 2.9 collective-permute-start.6
  88.3 2.9 dynamic-slice_dynamic-update-slice_fusion.2
  96.7 2.9 collective-permute-start.9
  102.5 2.9 collective-permute-start.12
  110.9 20.3 %collective-permute-done.9 = bf16[512,1024]{1,0:T(8,128)(2,1)S(1)} collective-permute-done((bf16[512,1024]{1,0:T(8,128)(2,1)S(1)}, bf16[512,1024]{1,0:T(8,128)(2,1)S(1)}, u32[]{:S(2)}, u32[]{:S(2)}) %collective-permute-start.9) | collective-permute-done | bytes 1048608 | tf_op jit(solution)/shard_map/ppermute | solution.py:48
  132.1 18.0 %collective-permute-done.12 = bf16[512,1024]{1,0:T(8,128)(2,1)S(1)} collective-permute-done((bf16[512,1024]{1,0:T(8,128)(2,1)S(1)}, bf16[512,1024]{1,0:T(8,128)(2,1)S(1)}, u32[]{:S(2)}, u32[]{:S(2)}) %collective-permute-start.12) | collective-permute-done | bytes 1048608 | tf_op jit(solution)/shard_map/ppermute | solution.py:48
  150.5 4.1 fusion.57
  155.6 3.9 fusion.54
  162.5 3.9 fusion.51
  166.5 3.9 fusion.48
  177.1 3.6 collective-permute-done.18
  182.1 10.0 %collective-permute-done.22 = bf16[256,1024]{1,0:T(8,128)(2,1)} collective-permute-done((bf16[256,1024]{1,0:T(8,128)(2,1)S(1)}, bf16[256,1024]{1,0:T(8,128)(2,1)}, u32[]{:S(2)}, u32[]{:S(2)}) %collective-permute-start.22) | collective-permute-done | bytes 524320 | tf_op jit(solution)/shard_map/ppermute | solution.py:15
  192.1 10.8 %collective-permute-done.26 = bf16[256,1024]{1,0:T(8,128)(2,1)} collective-permute-done((bf16[256,1024]{1,0:T(8,128)(2,1)S(1)}, bf16[256,1024]{1,0:T(8,128)(2,1)}, u32[]{:S(2)}, u32[]{:S(2)}) %collective-permute-start.26) | collective-permute-done | bytes 524320 | tf_op jit(solution)/shard_map/ppermute | solution.py:15
  206.3 2.8 convolution_add_fusion.1
  213.7 3.4 fusion.73
  225.2 2.8 fusion.75
  232.2 2.9 fusion.104
  235.9 3.0 fusion.106
  244.1 2.8 fusion.111
  246.9 2.9 fusion.113
  254.8 5.7 %collective-permute-done.43 = bf16[256,512]{1,0:T(8,128)(2,1)} collective-permute-done((bf16[256,512]{1,0:T(8,128)(2,1)S(1)}, bf16[256,512]{1,0:T(8,128)(2,1)}, u32[]{:S(2)}, u32[]{:S(2)}) %collective-permute-start.43) | collective-permute-done | bytes 262176 | tf_op jit(solution)/shard_map/ppermute | solution.py:15
  261.2 2.9 fusion.118
  264.1 3.8 collective-permute-done.45
  268.7 2.9 fusion.120
  271.6 3.1 collective-permute-done.47
  275.2 2.8 fusion.122
  278.0 3.1 collective-permute-done.49
  281.2 2.8 fusion.124
  301.0 2.8 fusion.105
  309.2 2.9 fusion.125
  312.1 3.5 collective-permute-start.31
  315.6 2.9 fusion.127
  328.9 6.2 %multiply_bitcast_fusion.3 = f32[1,512,1024]{2,1,0:T(8,128)S(1)} fusion(f32[512,1024]{1,0:T(8,128)} %fusion.110, f32[512,1024]{1,0:T(8,128)} %fusion.109, f32[512,1024]{1,0:T(8,128)} %fusion.108, f32[512,1024]{1,0:T(8,128)} %fusion.107, f32[512,1024]{1,0:T(8,128)} %fusion.106, f32[512,1024]{1,0:T(8,128)} %fusion.104, f32[512,1024]{1,0:T(8,128)} %fusion.105, ...), kind=kOutput, calls=%fused_computation.27 | convolution fusion | flops 273678336 | bytes 17569796 | tf_op jit(solution)/shard_map/dot_general | solution.py:19
  337.6 6.4 %collective-permute-done.46 = bf16[256,512]{1,0:T(8,128)(2,1)S(1)} collective-permute-done((bf16[256,512]{1,0:T(8,128)(2,1)}, bf16[256,512]{1,0:T(8,128)(2,1)S(1)}, u32[]{:S(2)}, u32[]{:S(2)}) %collective-permute-start.46) | collective-permute-done | bytes 262176 | tf_op jit(solution)/shard_map/ppermute | solution.py:15
  345.1 7.1 %collective-permute-done.48 = bf16[256,512]{1,0:T(8,128)(2,1)S(1)} collective-permute-done((bf16[256,512]{1,0:T(8,128)(2,1)}, bf16[256,512]{1,0:T(8,128)(2,1)S(1)}, u32[]{:S(2)}, u32[]{:S(2)}) %collective-permute-start.48) | collective-permute-done | bytes 262176 | tf_op jit(solution)/shard_map/ppermute | solution.py:15
  353.0 6.3 %collective-permute-done.50 = bf16[256,512]{1,0:T(8,128)(2,1)S(1)} collective-permute-done((bf16[256,512]{1,0:T(8,128)(2,1)S(1)}, bf16[256,512]{1,0:T(8,128)(2,1)S(1)}, u32[]{:S(2)}, u32[]{:S(2)}) %collective-permute-start.50) | collective-permute-done | bytes 262176 | tf_op jit(solution)/shard_map/ppermute | solution.py:15
  372.4 3.3 copy-done
  384.0 19.3 %collective-permute-done.62 = f16[512,1024]{1,0:T(8,128)(2,1)S(1)} collective-permute-done((f16[512,1024]{1,0:T(8,128)(2,1)}, f16[512,1024]{1,0:T(8,128)(2,1)S(1)}, u32[]{:S(2)}, u32[]{:S(2)}) %collective-permute-start.62) | collective-permute-done | bytes 1048608 | tf_op jit(solution)/shard_map/ppermute | solution.py:151
  403.3 3.3 fusion.11
  406.6 31.9 %collective-permute-start.63 = (f16[512,1024]{1,0:T(8,128)(2,1)S(1)}, f16[512,1024]{1,0:T(8,128)(2,1)S(1)}, u32[]{:S(2)}, u32[]{:S(2)}) collective-permute-start(f16[512,1024]{1,0:T(8,128)(2,1)S(1)} %get-tuple-element.21), channel_id=1, source_target_pairs={{0,8},{4,12},{8,16},{12,20},{1,9},{5,13},{9,17},{13,21},{2,10},{6,... | collective-permute-start | bytes 3145736 | tf_op jit(solution)/shard_map/ppermute | solution.py:151
  439.8 19.8 %collective-permute-done.63 = f16[512,1024]{1,0:T(8,128)(2,1)S(1)} collective-permute-done((f16[512,1024]{1,0:T(8,128)(2,1)S(1)}, f16[512,1024]{1,0:T(8,128)(2,1)S(1)}, u32[]{:S(2)}, u32[]{:S(2)}) %collective-permute-start.63) | collective-permute-done | bytes 1048608 | tf_op jit(solution)/shard_map/ppermute | solution.py:151
  461.5 4.5 collective-permute-start.64
  466.2 20.0 %collective-permute-done.64 = f16[512,1024]{1,0:T(8,128)(2,1)S(1)} collective-permute-done((f16[512,1024]{1,0:T(8,128)(2,1)S(1)}, f16[512,1024]{1,0:T(8,128)(2,1)S(1)}, u32[]{:S(2)}, u32[]{:S(2)}) %collective-permute-start.64) | collective-permute-done | bytes 1048608 | tf_op jit(solution)/shard_map/ppermute | solution.py:151
  486.2 3.6 fusion.15
  (250 shorter events, 144.2 us)
Async XLA Ops:
  0.6 28.3 %collective-permute-start.2 = (bf16[512,1024]{1,0:T(8,128)(2,1)}, bf16[512,1024]{1,0:T(8,128)(2,1)S(1)}, u32[]{:S(2)}, u32[]{:S(2)}) collective-permute-start(bf16[512,1024]{1,0:T(8,128)(2,1)} %param.5), channel_id=1, source_target_pairs={{8,0},{12,4},{16,8},{20,12},{24,16},{28,20},{9,1},{13,5},{17,9},{2... | collective-permute-start | bytes 3145736 | tf_op jit(solution)/shard_map/ppermute | solution.py:43
  1.9 28.3 %collective-permute-start.1 = (bf16[512,1024]{1,0:T(8,128)(2,1)}, bf16[512,1024]{1,0:T(8,128)(2,1)}, u32[]{:S(2)}, u32[]{:S(2)}) collective-permute-start(bf16[512,1024]{1,0:T(8,128)(2,1)} %param.5), channel_id=1, source_target_pairs={{0,8},{4,12},{8,16},{12,20},{16,24},{20,28},{1,9},{5,13},{9,17},{1... | collective-permute-start | bytes 3145736 | tf_op jit(solution)/shard_map/ppermute | solution.py:43
  28.9 26.2 %collective-permute-start.3 = (bf16[512,1024]{1,0:T(8,128)(2,1)S(1)}, bf16[512,1024]{1,0:T(8,128)(2,1)S(1)}, u32[]{:S(2)}, u32[]{:S(2)}) collective-permute-start(bf16[512,1024]{1,0:T(8,128)(2,1)S(1)} %collective-permute-done.2), channel_id=1, source_target_pairs={{8,0},{12,4},{16,8},{20,12},{9,1},{13,5},{17,9},{21,13},{10,2},{14... | collective-permute-start | bytes 3145736 | tf_op jit(solution)/shard_map/ppermute | solution.py:43
  30.2 38.5 %collective-permute-start.7 = (bf16[512,1024]{1,0:T(8,128)(2,1)}, bf16[512,1024]{1,0:T(8,128)(2,1)S(1)}, u32[]{:S(2)}, u32[]{:S(2)}) collective-permute-start(bf16[512,1024]{1,0:T(8,128)(2,1)} %collective-permute-done.1), channel_id=1, source_target_pairs={{8,16},{12,20},{16,24},{20,28},{9,17},{13,21},{17,25},{21,29},{10,... | collective-permute-start | bytes 3145736 | tf_op jit(solution)/shard_map/ppermute | solution.py:43
  55.2 25.4 %collective-permute-start.4 = (bf16[512,1024]{1,0:T(8,128)(2,1)S(1)}, bf16[512,1024]{1,0:T(8,128)(2,1)}, u32[]{:S(2)}, u32[]{:S(2)}) collective-permute-start(bf16[512,1024]{1,0:T(8,128)(2,1)S(1)} %collective-permute-done.3), channel_id=1, source_target_pairs={{8,0},{12,4},{9,1},{13,5},{10,2},{14,6},{11,3},{15,7}} | collective-permute-start | bytes 3145736 | tf_op jit(solution)/shard_map/ppermute | solution.py:43
  56.4 40.2 %collective-permute-start = (bf16[512,1024]{1,0:T(8,128)(2,1)}, bf16[512,1024]{1,0:T(8,128)(2,1)}, u32[]{:S(2)}, u32[]{:S(2)}) collective-permute-start(bf16[512,1024]{1,0:T(8,128)(2,1)} %param.5), channel_id=1, source_target_pairs={{0,4},{4,0},{8,12},{12,8},{16,20},{20,16},{24,28},{28,24},{1,5},{5... | collective-permute-start | bytes 3145736 | tf_op jit(solution)/shard_map/ppermute | solution.py:15
  67.1 35.5 %collective-permute-start.5 = (bf16[512,1024]{1,0:T(8,128)(2,1)}, bf16[512,1024]{1,0:T(8,128)(2,1)}, u32[]{:S(2)}, u32[]{:S(2)}) collective-permute-start(bf16[512,1024]{1,0:T(8,128)(2,1)} %collective-permute-done.1), channel_id=1, source_target_pairs={{8,12},{12,8},{16,20},{20,16},{24,28},{28,24},{9,13},{13,9},{17,21... | collective-permute-start | bytes 3145736 | tf_op jit(solution)/shard_map/ppermute | solution.py:48
  68.7 36.7 %collective-permute-start.10 = (bf16[512,1024]{1,0:T(8,128)(2,1)S(1)}, bf16[512,1024]{1,0:T(8,128)(2,1)}, u32[]{:S(2)}, u32[]{:S(2)}) collective-permute-start(bf16[512,1024]{1,0:T(8,128)(2,1)S(1)} %collective-permute-done.7), channel_id=1, source_target_pairs={{16,24},{20,28},{17,25},{21,29},{18,26},{22,30},{19,27},{23,31}} | collective-permute-start | bytes 3145736 | tf_op jit(solution)/shard_map/ppermute | solution.py:43
  80.6 28.3 %collective-permute-start.6 = (bf16[512,1024]{1,0:T(8,128)(2,1)}, bf16[512,1024]{1,0:T(8,128)(2,1)}, u32[]{:S(2)}, u32[]{:S(2)}) collective-permute-start(bf16[512,1024]{1,0:T(8,128)(2,1)} %collective-permute-done.4), channel_id=1, source_target_pairs={{0,4},{4,0},{1,5},{5,1},{2,6},{6,2},{3,7},{7,3}} | collective-permute-start | bytes 3145736 | tf_op jit(solution)/shard_map/ppermute | solution.py:48
  95.9 15.0 %collective-permute-start.8 = (bf16[512,1024]{1,0:T(8,128)(2,1)S(1)}, bf16[512,1024]{1,0:T(8,128)(2,1)S(1)}, u32[]{:S(2)}, u32[]{:S(2)}) collective-permute-start(bf16[512,1024]{1,0:T(8,128)(2,1)S(1)} %collective-permute-done.7), channel_id=1, source_target_pairs={{16,20},{20,16},{24,28},{28,24},{17,21},{21,17},{25,29},{29,25},{1... | collective-permute-start | bytes 3145736 | tf_op jit(solution)/shard_map/ppermute | solution.py:48
  96.7 34.6 %collective-permute-start.9 = (bf16[512,1024]{1,0:T(8,128)(2,1)S(1)}, bf16[512,1024]{1,0:T(8,128)(2,1)S(1)}, u32[]{:S(2)}, u32[]{:S(2)}) collective-permute-start(bf16[512,1024]{1,0:T(8,128)(2,1)S(1)} %collective-permute-done.3), channel_id=1, source_target_pairs={{0,4},{4,0},{8,12},{12,8},{1,5},{5,1},{9,13},{13,9},{2,6},{6,2},{1... | collective-permute-start | bytes 3145736 | tf_op jit(solution)/shard_map/ppermute | solution.py:48
  102.5 47.6 %collective-permute-start.12 = (bf16[512,1024]{1,0:T(8,128)(2,1)S(1)}, bf16[512,1024]{1,0:T(8,128)(2,1)S(1)}, u32[]{:S(2)}, u32[]{:S(2)}) collective-permute-start(bf16[512,1024]{1,0:T(8,128)(2,1)S(1)} %collective-permute-done.2), channel_id=1, source_target_pairs={{0,4},{4,0},{8,12},{12,8},{16,20},{20,16},{1,5},{5,1},{9,13},{13,9... | collective-permute-start | bytes 3145736 | tf_op jit(solution)/shard_map/ppermute | solution.py:48
  105.5 44.6 %collective-permute-start.11 = (bf16[512,1024]{1,0:T(8,128)(2,1)}, bf16[512,1024]{1,0:T(8,128)(2,1)S(1)}, u32[]{:S(2)}, u32[]{:S(2)}) collective-permute-start(bf16[512,1024]{1,0:T(8,128)(2,1)} %collective-permute-done.10), channel_id=1, source_target_pairs={{24,28},{28,24},{25,29},{29,25},{26,30},{30,26},{27,31},{31,27}} | collective-permute-start | bytes 3145736 | tf_op jit(solution)/shard_map/ppermute | solution.py:48
  154.7 17.8 %collective-permute-start.13 = (bf16[256,1024]{1,0:T(8,128)(2,1)S(1)}, bf16[256,1024]{1,0:T(8,128)(2,1)S(1)}, u32[]{:S(2)}, u32[]{:S(2)}) collective-permute-start(bf16[256,1024]{1,0:T(8,128)(2,1)S(1)} %fusion.57), channel_id=1, source_target_pairs={{0,1},{1,0},{2,3},{3,2},{4,5},{5,4},{6,7},{7,6},{8,9},{9,8},{10,11... | collective-permute-start | bytes 1572872 | tf_op jit(solution)/shard_map/ppermute | solution.py:15
  154.8 20.2 %collective-permute-start.14 = (bf16[256,1024]{1,0:T(8,128)(2,1)S(1)}, bf16[256,1024]{1,0:T(8,128)(2,1)S(1)}, u32[]{:S(2)}, u32[]{:S(2)}) collective-permute-start(bf16[256,1024]{1,0:T(8,128)(2,1)S(1)} %fusion.57), channel_id=1, source_target_pairs={{0,2},{1,3},{2,0},{3,1},{4,6},{5,7},{6,4},{7,5},{8,10},{9,11},{10,... | collective-permute-start | bytes 1572872 | tf_op jit(solution)/shard_map/ppermute | solution.py:15
  161.0 13.0 %collective-permute-start.17 = (bf16[256,1024]{1,0:T(8,128)(2,1)S(1)}, bf16[256,1024]{1,0:T(8,128)(2,1)S(1)}, u32[]{:S(2)}, u32[]{:S(2)}) collective-permute-start(bf16[256,1024]{1,0:T(8,128)(2,1)S(1)} %fusion.54), channel_id=1, source_target_pairs={{0,1},{1,0},{2,3},{3,2},{4,5},{5,4},{6,7},{7,6},{8,9},{9,8},{10,11... | collective-permute-start | bytes 1572872 | tf_op jit(solution)/shard_map/ppermute | solution.py:15
  161.3 19.5 %collective-permute-start.18 = (bf16[256,1024]{1,0:T(8,128)(2,1)S(1)}, bf16[256,1024]{1,0:T(8,128)(2,1)S(1)}, u32[]{:S(2)}, u32[]{:S(2)}) collective-permute-start(bf16[256,1024]{1,0:T(8,128)(2,1)S(1)} %fusion.54), channel_id=1, source_target_pairs={{0,2},{1,3},{2,0},{3,1},{4,6},{5,7},{6,4},{7,5},{8,10},{9,11},{10,... | collective-permute-start | bytes 1572872 | tf_op jit(solution)/shard_map/ppermute | solution.py:15
  170.4 11.2 %collective-permute-start.21 = (bf16[256,1024]{1,0:T(8,128)(2,1)S(1)}, bf16[256,1024]{1,0:T(8,128)(2,1)S(1)}, u32[]{:S(2)}, u32[]{:S(2)}) collective-permute-start(bf16[256,1024]{1,0:T(8,128)(2,1)S(1)} %fusion.51), channel_id=1, source_target_pairs={{0,1},{1,0},{2,3},{3,2},{4,5},{5,4},{6,7},{7,6},{8,9},{9,8},{10,11... | collective-permute-start | bytes 1572872 | tf_op jit(solution)/shard_map/ppermute | solution.py:15
  172.5 19.7 %collective-permute-start.22 = (bf16[256,1024]{1,0:T(8,128)(2,1)S(1)}, bf16[256,1024]{1,0:T(8,128)(2,1)}, u32[]{:S(2)}, u32[]{:S(2)}) collective-permute-start(bf16[256,1024]{1,0:T(8,128)(2,1)S(1)} %fusion.51), channel_id=1, source_target_pairs={{0,2},{1,3},{2,0},{3,1},{4,6},{5,7},{6,4},{7,5},{8,10},{9,11},{10,... | collective-permute-start | bytes 1572872 | tf_op jit(solution)/shard_map/ppermute | solution.py:15
  174.0 31.5 %collective-permute-start.25 = (bf16[256,1024]{1,0:T(8,128)(2,1)S(1)}, bf16[256,1024]{1,0:T(8,128)(2,1)S(1)}, u32[]{:S(2)}, u32[]{:S(2)}) collective-permute-start(bf16[256,1024]{1,0:T(8,128)(2,1)S(1)} %fusion.48), channel_id=1, source_target_pairs={{0,1},{1,0},{2,3},{3,2},{4,5},{5,4},{6,7},{7,6},{8,9},{9,8},{10,11... | collective-permute-start | bytes 1572872 | tf_op jit(solution)/shard_map/ppermute | solution.py:15
  175.0 27.9 %collective-permute-start.26 = (bf16[256,1024]{1,0:T(8,128)(2,1)S(1)}, bf16[256,1024]{1,0:T(8,128)(2,1)}, u32[]{:S(2)}, u32[]{:S(2)}) collective-permute-start(bf16[256,1024]{1,0:T(8,128)(2,1)S(1)} %fusion.48), channel_id=1, source_target_pairs={{0,2},{1,3},{2,0},{3,1},{4,6},{5,7},{6,4},{7,5},{8,10},{9,11},{10,... | collective-permute-start | bytes 1572872 | tf_op jit(solution)/shard_map/ppermute | solution.py:15
  180.8 28.3 %collective-permute-start.15 = (bf16[256,1024]{1,0:T(8,128)(2,1)S(1)}, bf16[256,1024]{1,0:T(8,128)(2,1)S(1)}, u32[]{:S(2)}, u32[]{:S(2)}) collective-permute-start(bf16[256,1024]{1,0:T(8,128)(2,1)S(1)} %collective-permute-done.14), channel_id=1, source_target_pairs={{0,1},{1,0},{2,3},{3,2},{4,5},{5,4},{6,7},{7,6},{8,9},{9,8},{10,11... | collective-permute-start | bytes 1572872 | tf_op jit(solution)/shard_map/ppermute | solution.py:15
  181.6 32.1 %collective-permute-start.19 = (bf16[256,1024]{1,0:T(8,128)(2,1)S(1)}, bf16[256,1024]{1,0:T(8,128)(2,1)}, u32[]{:S(2)}, u32[]{:S(2)}) collective-permute-start(bf16[256,1024]{1,0:T(8,128)(2,1)S(1)} %collective-permute-done.18), channel_id=1, source_target_pairs={{0,1},{1,0},{2,3},{3,2},{4,5},{5,4},{6,7},{7,6},{8,9},{9,8},{10,11... | collective-permute-start | bytes 1572872 | tf_op jit(solution)/shard_map/ppermute | solution.py:15
  192.1 28.5 %collective-permute-start.23 = (bf16[256,1024]{1,0:T(8,128)(2,1)}, bf16[256,1024]{1,0:T(8,128)(2,1)}, u32[]{:S(2)}, u32[]{:S(2)}) collective-permute-start(bf16[256,1024]{1,0:T(8,128)(2,1)} %collective-permute-done.22), channel_id=1, source_target_pairs={{0,1},{1,0},{2,3},{3,2},{4,5},{5,4},{6,7},{7,6},{8,9},{9,8},{10,11... | collective-permute-start | bytes 1572872 | tf_op jit(solution)/shard_map/ppermute | solution.py:15
  202.9 22.3 %collective-permute-start.27 = (bf16[256,1024]{1,0:T(8,128)(2,1)}, bf16[256,1024]{1,0:T(8,128)(2,1)}, u32[]{:S(2)}, u32[]{:S(2)}) collective-permute-start(bf16[256,1024]{1,0:T(8,128)(2,1)} %collective-permute-done.26), channel_id=1, source_target_pairs={{0,1},{1,0},{2,3},{3,2},{4,5},{5,4},{6,7},{7,6},{8,9},{9,8},{10,11... | collective-permute-start | bytes 1572872 | tf_op jit(solution)/shard_map/ppermute | solution.py:15
  210.7 73.3 %collective-permute-start.16 = (bf16[256,1024]{1,0:T(8,128)(2,1)}, bf16[256,1024]{1,0:T(8,128)(2,1)S(1)}, u32[]{:S(2)}, u32[]{:S(2)}) collective-permute-start(bf16[256,1024]{1,0:T(8,128)(2,1)} %get-tuple-element.44), channel_id=1, source_target_pairs={{0,4},{4,0},{8,12},{12,8},{16,20},{20,16},{24,28},{28,24},{1,5},{5... | collective-permute-start | bytes 1572872 | tf_op jit(solution)/shard_map/ppermute | solution.py:15
  217.1 67.6 %collective-permute-start.20 = (bf16[256,1024]{1,0:T(8,128)(2,1)}, bf16[256,1024]{1,0:T(8,128)(2,1)S(1)}, u32[]{:S(2)}, u32[]{:S(2)}) collective-permute-start(bf16[256,1024]{1,0:T(8,128)(2,1)} %get-tuple-element.45), channel_id=1, source_target_pairs={{0,4},{4,0},{8,12},{12,8},{16,20},{20,16},{24,28},{28,24},{1,5},{5... | collective-permute-start | bytes 1572872 | tf_op jit(solution)/shard_map/ppermute | solution.py:15
  223.2 61.7 %collective-permute-start.24 = (bf16[256,1024]{1,0:T(8,128)(2,1)S(1)}, bf16[256,1024]{1,0:T(8,128)(2,1)S(1)}, u32[]{:S(2)}, u32[]{:S(2)}) collective-permute-start(bf16[256,1024]{1,0:T(8,128)(2,1)S(1)} %get-tuple-element.43), channel_id=1, source_target_pairs={{0,4},{4,0},{8,12},{12,8},{16,20},{20,16},{24,28},{28,24},{1,5},{5... | collective-permute-start | bytes 1572872 | tf_op jit(solution)/shard_map/ppermute | solution.py:15
  228.0 57.6 %collective-permute-start.28 = (bf16[256,1024]{1,0:T(8,128)(2,1)S(1)}, bf16[256,1024]{1,0:T(8,128)(2,1)S(1)}, u32[]{:S(2)}, u32[]{:S(2)}) collective-permute-start(bf16[256,1024]{1,0:T(8,128)(2,1)S(1)} %get-tuple-element.42), channel_id=1, source_target_pairs={{0,4},{4,0},{8,12},{12,8},{16,20},{20,16},{24,28},{28,24},{1,5},{5... | collective-permute-start | bytes 1572872 | tf_op jit(solution)/shard_map/ppermute | solution.py:15
  235.1 8.5 %collective-permute-start.35 = (bf16[256,512]{1,0:T(8,128)(2,1)S(1)}, bf16[256,512]{1,0:T(8,128)(2,1)S(1)}, u32[]{:S(2)}, u32[]{:S(2)}) collective-permute-start(bf16[256,512]{1,0:T(8,128)(2,1)S(1)} %bitcast.176), channel_id=1, source_target_pairs={{0,1},{1,0},{2,3},{3,2},{4,5},{5,4},{6,7},{7,6},{8,9},{9,8},{10,11... | collective-permute-start | bytes 786440 | tf_op jit(solution)/shard_map/ppermute | solution.py:15
  252.1 8.3 %collective-permute-start.43 = (bf16[256,512]{1,0:T(8,128)(2,1)S(1)}, bf16[256,512]{1,0:T(8,128)(2,1)}, u32[]{:S(2)}, u32[]{:S(2)}) collective-permute-start(bf16[256,512]{1,0:T(8,128)(2,1)S(1)} %bitcast.177), channel_id=1, source_target_pairs={{0,2},{1,3},{2,0},{3,1},{4,6},{5,7},{6,4},{7,5},{8,10},{9,11},{10,... | collective-permute-start | bytes 786440 | tf_op jit(solution)/shard_map/ppermute | solution.py:15
  281.2 28.1 %collective-permute-start.51 = (bf16[256,512]{1,0:T(8,128)(2,1)}, bf16[256,512]{1,0:T(8,128)(2,1)}, u32[]{:S(2)}, u32[]{:S(2)}) collective-permute-start(bf16[256,512]{1,0:T(8,128)(2,1)} %collective-permute-done.43), channel_id=1, source_target_pairs={{0,1},{1,0},{2,3},{3,2},{4,5},{5,4},{6,7},{7,6},{8,9},{9,8},{10,11... | collective-permute-start | bytes 786440 | tf_op jit(solution)/shard_map/ppermute | solution.py:15
  284.0 28.2 %collective-permute-start.53 = (bf16[256,512]{1,0:T(8,128)(2,1)}, bf16[256,512]{1,0:T(8,128)(2,1)}, u32[]{:S(2)}, u32[]{:S(2)}) collective-permute-start(bf16[256,512]{1,0:T(8,128)(2,1)} %collective-permute-done.45), channel_id=1, source_target_pairs={{0,1},{1,0},{2,3},{3,2},{4,5},{5,4},{6,7},{7,6},{8,9},{9,8},{10,11... | collective-permute-start | bytes 786440 | tf_op jit(solution)/shard_map/ppermute | solution.py:15
  284.7 34.6 %collective-permute-start.55 = (bf16[256,512]{1,0:T(8,128)(2,1)}, bf16[256,512]{1,0:T(8,128)(2,1)}, u32[]{:S(2)}, u32[]{:S(2)}) collective-permute-start(bf16[256,512]{1,0:T(8,128)(2,1)} %collective-permute-done.47), channel_id=1, source_target_pairs={{0,1},{1,0},{2,3},{3,2},{4,5},{5,4},{6,7},{7,6},{8,9},{9,8},{10,11... | collective-permute-start | bytes 786440 | tf_op jit(solution)/shard_map/ppermute | solution.py:15
  284.9 37.7 %collective-permute-start.57 = (bf16[256,512]{1,0:T(8,128)(2,1)}, bf16[256,512]{1,0:T(8,128)(2,1)}, u32[]{:S(2)}, u32[]{:S(2)}) collective-permute-start(bf16[256,512]{1,0:T(8,128)(2,1)} %collective-permute-done.49), channel_id=1, source_target_pairs={{0,1},{1,0},{2,3},{3,2},{4,5},{5,4},{6,7},{7,6},{8,9},{9,8},{10,11... | collective-permute-start | bytes 786440 | tf_op jit(solution)/shard_map/ppermute | solution.py:15
  287.1 31.4 %collective-permute-start.29 = (f32[1152]{0:T(1024)S(1)}, f32[1152]{0:T(1024)S(1)}, u32[]{:S(2)}, u32[]{:S(2)}) collective-permute-start(f32[1152]{0:T(1024)S(1)} %concatenate.11), channel_id=1, source_target_pairs={{0,8},{4,12},{8,16},{12,20},{16,24},{20,28},{24,0},{28,4},{1,9},{5... | collective-permute-start | bytes 13832 | tf_op jit(solution)/shard_map/ppermute | solution.py:103
  309.2 9.3 %collective-permute-start.30 = (f32[1152]{0:T(1024)S(1)}, f32[1152]{0:T(1024)S(1)}, u32[]{:S(2)}, u32[]{:S(2)}) collective-permute-start(f32[1152]{0:T(1024)S(1)} %concatenate.11), channel_id=1, source_target_pairs={{0,16},{4,20},{8,24},{12,28},{16,0},{20,4},{24,8},{28,12},{1,17},{... | collective-permute-start | bytes 13832 | tf_op jit(solution)/shard_map/ppermute | solution.py:103
  318.5 41.7 %collective-permute-start.36 = (bf16[256,512]{1,0:T(8,128)(2,1)}, bf16[256,512]{1,0:T(8,128)(2,1)}, u32[]{:S(2)}, u32[]{:S(2)}) collective-permute-start(bf16[256,512]{1,0:T(8,128)(2,1)} %bitcast.162), channel_id=1, source_target_pairs={{0,1},{1,0},{2,3},{3,2},{4,5},{5,4},{6,7},{7,6},{8,9},{9,8},{10,11... | collective-permute-start | bytes 786440 | tf_op jit(solution)/shard_map/ppermute | solution.py:15
  318.5 43.8 %collective-permute-start.38 = (bf16[256,512]{1,0:T(8,128)(2,1)}, bf16[256,512]{1,0:T(8,128)(2,1)}, u32[]{:S(2)}, u32[]{:S(2)}) collective-permute-start(bf16[256,512]{1,0:T(8,128)(2,1)} %bitcast.160), channel_id=1, source_target_pairs={{0,1},{1,0},{2,3},{3,2},{4,5},{5,4},{6,7},{7,6},{8,9},{9,8},{10,11... | collective-permute-start | bytes 786440 | tf_op jit(solution)/shard_map/ppermute | solution.py:15
  319.1 44.9 %collective-permute-start.40 = (bf16[256,512]{1,0:T(8,128)(2,1)}, bf16[256,512]{1,0:T(8,128)(2,1)}, u32[]{:S(2)}, u32[]{:S(2)}) collective-permute-start(bf16[256,512]{1,0:T(8,128)(2,1)} %bitcast.158), channel_id=1, source_target_pairs={{0,1},{1,0},{2,3},{3,2},{4,5},{5,4},{6,7},{7,6},{8,9},{9,8},{10,11... | collective-permute-start | bytes 786440 | tf_op jit(solution)/shard_map/ppermute | solution.py:15
  325.9 9.2 %collective-permute-start.44 = (bf16[256,512]{1,0:T(8,128)(2,1)}, bf16[256,512]{1,0:T(8,128)(2,1)}, u32[]{:S(2)}, u32[]{:S(2)}) collective-permute-start(bf16[256,512]{1,0:T(8,128)(2,1)} %bitcast.162), channel_id=1, source_target_pairs={{0,2},{1,3},{2,0},{3,1},{4,6},{5,7},{6,4},{7,5},{8,10},{9,11},{10,... | collective-permute-start | bytes 786440 | tf_op jit(solution)/shard_map/ppermute | solution.py:15
  327.4 38.7 %collective-permute-start.42 = (bf16[256,512]{1,0:T(8,128)(2,1)S(1)}, bf16[256,512]{1,0:T(8,128)(2,1)S(1)}, u32[]{:S(2)}, u32[]{:S(2)}) collective-permute-start(bf16[256,512]{1,0:T(8,128)(2,1)S(1)} %bitcast.166), channel_id=1, source_target_pairs={{0,1},{1,0},{2,3},{3,2},{4,5},{5,4},{6,7},{7,6},{8,9},{9,8},{10,11... | collective-permute-start | bytes 786440 | tf_op jit(solution)/shard_map/ppermute | solution.py:15
  335.1 9.0 %collective-permute-start.46 = (bf16[256,512]{1,0:T(8,128)(2,1)}, bf16[256,512]{1,0:T(8,128)(2,1)S(1)}, u32[]{:S(2)}, u32[]{:S(2)}) collective-permute-start(bf16[256,512]{1,0:T(8,128)(2,1)} %bitcast.160), channel_id=1, source_target_pairs={{0,2},{1,3},{2,0},{3,1},{4,6},{5,7},{6,4},{7,5},{8,10},{9,11},{10,... | collective-permute-start | bytes 786440 | tf_op jit(solution)/shard_map/ppermute | solution.py:15
  377.8 25.5 %collective-permute-start.62 = (f16[512,1024]{1,0:T(8,128)(2,1)}, f16[512,1024]{1,0:T(8,128)(2,1)S(1)}, u32[]{:S(2)}, u32[]{:S(2)}) collective-permute-start(f16[512,1024]{1,0:T(8,128)(2,1)} %get-tuple-element.23), channel_id=1, source_target_pairs={{0,8},{4,12},{1,9},{5,13},{2,10},{6,14},{3,11},{7,15}} | collective-permute-start | bytes 3145736 | tf_op jit(solution)/shard_map/ppermute | solution.py:151
  382.4 20.9 %collective-permute-start.60 = (f16[512,1024]{1,0:T(8,128)(2,1)S(1)}, f16[512,1024]{1,0:T(8,128)(2,1)}, u32[]{:S(2)}, u32[]{:S(2)}) collective-permute-start(f16[512,1024]{1,0:T(8,128)(2,1)S(1)} %fusion.10), channel_id=1, source_target_pairs={{24,16},{28,20},{16,8},{20,12},{25,17},{29,21},{17,9},{21,13},{26,... | collective-permute-start | bytes 3145736 | tf_op jit(solution)/shard_map/ppermute | solution.py:151
  406.6 53.0 %collective-permute-start.63 = (f16[512,1024]{1,0:T(8,128)(2,1)S(1)}, f16[512,1024]{1,0:T(8,128)(2,1)S(1)}, u32[]{:S(2)}, u32[]{:S(2)}) collective-permute-start(f16[512,1024]{1,0:T(8,128)(2,1)S(1)} %get-tuple-element.21), channel_id=1, source_target_pairs={{0,8},{4,12},{8,16},{12,20},{1,9},{5,13},{9,17},{13,21},{2,10},{6,... | collective-permute-start | bytes 3145736 | tf_op jit(solution)/shard_map/ppermute | solution.py:151
  438.5 27.7 %collective-permute-start.61 = (f16[512,1024]{1,0:T(8,128)(2,1)S(1)}, f16[512,1024]{1,0:T(8,128)(2,1)S(1)}, u32[]{:S(2)}, u32[]{:S(2)}) collective-permute-start(f16[512,1024]{1,0:T(8,128)(2,1)S(1)} %get-tuple-element.20), channel_id=1, source_target_pairs={{24,16},{28,20},{16,8},{20,12},{8,0},{12,4},{25,17},{29,21},{17,9}... | collective-permute-start | bytes 3145736 | tf_op jit(solution)/shard_map/ppermute | solution.py:151
  461.5 24.7 %collective-permute-start.64 = (f16[512,1024]{1,0:T(8,128)(2,1)S(1)}, f16[512,1024]{1,0:T(8,128)(2,1)S(1)}, u32[]{:S(2)}, u32[]{:S(2)}) collective-permute-start(f16[512,1024]{1,0:T(8,128)(2,1)S(1)} %fusion.9), channel_id=1, source_target_pairs={{0,8},{4,12},{8,16},{12,20},{16,24},{20,28},{1,9},{5,13},{9,17},{1... | collective-permute-start | bytes 3145736 | tf_op jit(solution)/shard_map/ppermute | solution.py:151
  (38 other events, 277.3 us)
